TPU v7x, 256 devices: a whole 4x4x8 slice. The times are simulated.
256 devices in a mesh: seq: 64 (over z, y, core), head: 4 (over x).
Axes of the slice: x: 4, y: 4, z: 8, core: 2. Of those that a mesh axis runs over, the one named last changes fastest.
Arguments:
- queries: bfloat16 [65536, 512], P('seq', 'head'), may hold values from -8 to 8
- key_rows: bfloat16 [65536, 512], P('seq', 'head'), may hold values from -8 to 8
- value_rows: bfloat16 [65536, 512], P('seq', 'head'), may hold values from -24 to 24
- offsets: int32 [4, 8], P(None, 'head'), may hold values from 0 to 7
- w_out: bfloat16 [512, 1024], P('head'), may hold values from -0.25 to 0.25
- d_out: bfloat16 [65536, 1024], P('seq', 'head'), may hold values from -6 to 6
Outputs:
- layer_out: bfloat16 [65536, 1024], P('seq', 'head')
- q_grad: bfloat16 [65536, 512], P('seq', 'head')
- k_grad: bfloat16 [65536, 512], P('seq', 'head')
- v_grad: bfloat16 [65536, 512], P('seq', 'head')
Inputs may be any that keep to these rules, and one draw needn't show every extreme that they name: The offset of head h at level l is offsets[l, h] mod 2^l.
All inputs are finite; a program needn't handle non-finite values.
Results may differ from a plain program's by a relative error of at most 0.03.
Values may be sent and summed in bfloat16 or wider, within the bound.
A program may use at most 128 MiB of HBM per device.

v0:
```python
import functools

import jax
import jax.numpy as jnp
from jax import lax
from jax.experimental import pallas as pl
from jax.experimental.pallas import tpu as pltpu
from jax.sharding import PartitionSpec as P

MESH = pl.DeviceIdType.MESH
HD = 64
LEVELS = 4
T = 1024
C = 128
FIRST = (0, 8, 12, 14)
COUNT = (8, 4, 2, 1)
BLOCKS = 15
F32, BF16 = jnp.float32, jnp.bfloat16


def nn(a, b):
    return lax.dot_general(a, b, (((1,), (0,)), ((), ())), preferred_element_type=F32)


def nt(a, b):
    return lax.dot_general(a, b, (((1,), (1,)), ((), ())), preferred_element_type=F32)


def iota(shape, dim):
    return lax.broadcasted_iota(jnp.int32, shape, dim)


def split3(x):
    hi = x.astype(BF16)
    rest = x - hi.astype(F32)
    mid = rest.astype(BF16)
    lo = (rest - mid.astype(F32)).astype(BF16)
    return hi.astype(F32), mid.astype(F32), lo.astype(F32)


def pick_row(row, values):
    out = jnp.zeros_like(values[0] + row.astype(F32))
    for i, value in enumerate(values):
        out = jnp.where(row == i, value, out)
    return out


def kernel(
    nh,
    off,
    q_ref,
    k_ref,
    v_ref,
    w_ref,
    g_ref,
    layer_ref,
    dq_ref,
    dk_ref,
    dv_ref,
    sel1,
    sel2,
    sel3,
    qt,
    kvo,
    kvt,
    qbd,
    dbd,
    probs,
    mst,
    kvs1,
    kvs2,
    kvs3,
    wfull,
    dsend,
    drecv,
    dap,
    toko,
    tokl,
    att,
    qacc,
    dkv,
    gs1,
    gs2,
    gs3,
    gr1,
    gr2,
    gr3,
    own1,
    own2,
    own3,
    kv_ss,
    kv_rs,
    gr_ss,
    gr_rs,
    w_ss,
    w_rs,
    d_ss,
    d_rs,
    a_ss,
    a_rs,
):
    sels = (None, sel1, sel2, sel3)
    kvs = (None, kvs1, kvs2, kvs3)
    gsend = (None, gs1, gs2, gs3)
    grecv = (None, gr1, gr2, gr3)
    owns = (None, own1, own2, own3)
    seq = lax.axis_index("seq")
    hx = lax.axis_index("head")
    rank = [lax.rem(seq, 1 << l) for l in range(LEVELS)]

    def member(l, d):
        return seq - rank[l] + lax.rem(rank[l] + d, 1 << l)

    def slot(l, d):
        return (1 << l) - 2 - l + 1 + d - 1 if l else 0

    def head_peer(d):
        return lax.rem(hx + d, nh)

    barrier = pltpu.get_barrier_semaphore()
    for d in range(1, 8):
        pl.semaphore_signal(barrier, inc=1, device_id=(member(3, d), hx), device_id_type=MESH)
    for d in range(1, nh):
        pl.semaphore_signal(barrier, inc=1, device_id=(seq, head_peer(d)), device_id_type=MESH)
    pl.semaphore_wait(barrier, 7 + nh - 1)

    def w_copy(d):
        return pltpu.make_async_remote_copy(
            src_ref=w_ref.at[:, pl.ds(pl.multiple_of(head_peer(d) * 256, 256), 256)],
            dst_ref=wfull.at[pl.ds(pl.multiple_of(hx * 128, 128), 128), :],
            send_sem=w_ss.at[d - 1],
            recv_sem=w_rs.at[d - 1],
            device_id=(seq, head_peer(d)),
            device_id_type=MESH,
        )

    for d in range(1, nh):
        w_copy(d).start()
    own_w = pl.ds(pl.multiple_of(hx * 128, 128), 128)
    wfull[own_w, :] = w_ref[:, pl.ds(pl.multiple_of(hx * 256, 256), 256)]

    lane = iota((1, 256), 1)
    second = lane >= C
    offs = [[lax.rem(off[l, h], 1 << l) for h in range(2)] for l in range(LEVELS)]

    def kv_copy(l, d):
        n = T >> l
        i = slot(l, d)
        return pltpu.make_async_remote_copy(
            src_ref=kvs[l],
            dst_ref=kvo.at[l, pl.ds(pl.multiple_of(rank[l] * n, n), n), pl.ds(0, 256)],
            send_sem=kv_ss.at[i],
            recv_sem=kv_rs.at[i],
            device_id=(member(l, d), hx),
            device_id_type=MESH,
        )

    kv0 = jnp.concatenate([k_ref[...], v_ref[...]], axis=1)
    kvo[0, :, 0:256] = kv0
    kvo[:, :, 256:384] = jnp.ones((LEVELS, T, 128), BF16)
    kv_head1 = lax.rem(iota((C, 256), 1), 128) >= HD
    for l in (1, 2, 3):
        r = 1 << l
        tok = C * r
        n = T >> l
        row2 = iota((256, tok), 0)
        target = lax.rem(row2, C) * r + jnp.where(row2 >= C, offs[l][1], offs[l][0])
        selt = jnp.where(iota((256, tok), 1) == target, 1.0, 0.0).astype(BF16)
        for c in range(COUNT[l]):
            both = nn(selt, kvo[0, c * tok : (c + 1) * tok, 0:256])
            kvs[l][c * C : (c + 1) * C, :] = jnp.where(kv_head1, both[C:], both[:C]).astype(BF16)
        for d in range(1, r):
            kv_copy(l, d).start()
        kvo[l, pl.ds(pl.multiple_of(rank[l] * n, n), n), 0:256] = kvs[l][...]
        target = lax.rem(lane, C) * r + jnp.where(second, offs[l][1], offs[l][0])
        sels[l][...] = jnp.where(iota((tok, 256), 0) == target, 1.0, 0.0).astype(BF16)

    eye = jnp.where(iota((256, 256), 0) == iota((256, 256), 1), 1.0, 0.0).astype(BF16)
    diag = (iota((C, 256), 0) >= HD) == (iota((C, 256), 1) >= C)
    qt[...] = (nt(eye[:C, :C], q_ref[...]) * 0.125).astype(BF16)
    for l in range(LEVELS):
        tok = C << l
        for c in range(COUNT[l]):
            part = qt[:, c * tok : (c + 1) * tok]
            if l == 0:
                both = jnp.concatenate([part, part], axis=1).astype(F32)
            else:
                both = nn(part, sels[l][...])
            qbd[FIRST[l] + c] = jnp.where(diag, both, 0.0).astype(BF16)
    dbd[:, 144:256, :] = jnp.zeros((BLOCKS, 112, 256), BF16)
    kvt[:, 256:272, :] = jnp.ones((LEVELS, 16, T), BF16)

    row16 = iota((16, 256), 0)
    own_row = lax.div(row16, 3) == lax.div(iota((16, 256), 1), C)
    top = iota((C, C), 0) < HD

    def transpose_kv(l):
        for c in range(4):
            rows = slice(c * 256, (c + 1) * 256)
            kvt[l, 0:256, rows] = nt(eye, kvo[l, rows, 0:256]).astype(BF16)

    def forward_block(l, c):
        b = FIRST[l] + c
        score = nn(kvo[l, :, 0:128], qbd[b])
        top_score = jnp.max(score, axis=0, keepdims=True)
        prob = jnp.exp(score - top_score).astype(BF16)
        probs[b] = prob
        out = nn(kvt[l, 128:272, :], prob)
        total = out[C : C + 1]
        lse = top_score + jnp.log(total)
        mst[b, 0:1, :] = top_score
        out = out[:C] * (1.0 / total)
        if l == 0:
            where = pl.ds(pl.multiple_of(c * C, C), C)
            toko[0, :, where] = jnp.where(top, out[:, :C], out[:, C:])
            tokl[0, 0:1, where] = lse[:, :C]
            tokl[0, 1:2, where] = lse[:, C:]
            return
        r = 1 << l
        tok = C * r
        where = pl.ds(pl.multiple_of(c * tok, tok), tok)
        pieces = pick_row(lax.rem(row16, 3), split3(lse))
        pieces = jnp.where(own_row, pieces, 0.0)
        packed = jnp.concatenate([jnp.where(diag, out, 0.0), pieces], axis=0).astype(BF16)
        placed = nt(packed, sels[l][...])
        toko[l, :, where] = placed[:C]
        phase = lax.rem(iota((1, tok), 1), r)
        for h in range(2):
            i = C + 3 * h
            value = placed[i : i + 1] + placed[i + 1 : i + 2] + placed[i + 2 : i + 3]
            tokl[l, h : h + 1, where] = jnp.where(phase == offs[l][h], value, -1e30)

    def forward_level(l, first, last):
        if last - first == 1:
            forward_block(l, first)
        else:
            pl.loop(first, last)(lambda c: forward_block(l, c))

    def d_copy(d):
        return pltpu.make_async_remote_copy(
            src_ref=dsend.at[pl.ds(pl.multiple_of(head_peer(d) * 128, 128), 128), :],
            dst_ref=drecv.at[d - 1],
            send_sem=d_ss.at[d - 1],
            recv_sem=d_rs.at[d - 1],
            device_id=(seq, head_peer(d)),
            device_id_type=MESH,
        )

    transpose_kv(0)
    forward_level(0, 0, 4)
    for d in range(1, nh):
        w_copy(d).wait_recv()
    for c in range(4):
        cols = slice(c * 256, (c + 1) * 256)
        dsend[:, cols] = nt(wfull[...], g_ref[cols, :]).astype(BF16)
    for d in range(1, nh):
        d_copy(d).start()
    forward_level(0, 4, 8)
    for l in (1, 2, 3):
        for d in range(1, 1 << l):
            kv_copy(l, d).wait_recv()
        transpose_kv(l)
        forward_level(l, 0, COUNT[l])

    lses = [tokl[l, 0:2, :] for l in range(LEVELS)]
    peak = jnp.maximum(jnp.maximum(lses[0], lses[1]), jnp.maximum(lses[2], lses[3]))
    total = sum(jnp.exp(x - peak) for x in lses)
    joint = peak + jnp.log(total)
    is_top = iota((C, T), 0) < HD
    mixed = jnp.zeros((C, T), F32)
    for l in range(LEVELS):
        weight = jnp.exp(lses[l] - joint)
        mixed = mixed + jnp.where(is_top, weight[0:1], weight[1:2]) * toko[l]
    mixed_b = mixed.astype(BF16)
    dap[128:256, :] = mixed_b
    own_cols = pl.ds(pl.multiple_of(hx * 128, 128), 128)
    att[:, own_cols] = mixed_b.astype(F32).T.astype(BF16)
    rowt = iota((16, T), 0)
    hi, mid, lo = split3(joint)
    dap[256:272, :] = pick_row(
        rowt, (hi[0:1], mid[0:1], lo[0:1], hi[1:2], mid[1:2], lo[1:2])
    ).astype(BF16)

    def a_copy(d):
        return pltpu.make_async_remote_copy(
            src_ref=att.at[:, own_cols],
            dst_ref=att.at[:, own_cols],
            send_sem=a_ss.at[d - 1],
            recv_sem=a_rs.at[d - 1],
            device_id=(seq, head_peer(d)),
            device_id_type=MESH,
        )

    for d in range(1, nh):
        a_copy(d).start()

    d_sum = dsend[pl.ds(pl.multiple_of(hx * 128, 128), 128), :].astype(F32)
    for d in range(1, nh):
        d_copy(d).wait_recv()
        d_sum = d_sum + drecv[d - 1].astype(F32)
    dap[0:128, :] = d_sum.astype(BF16)

    def prepare(l, c):
        b = FIRST[l] + c
        tok = C << l
        part = dap[:, c * tok : (c + 1) * tok]
        if l == 0:
            both = jnp.concatenate([part, part], axis=1).astype(F32)
        else:
            both = nn(part, sels[l][...])
        x = both[256:272]
        lse = jnp.where(second, x[3:4] + x[4:5] + x[5:6], x[0:1] + x[1:2] + x[2:3])
        coef = jnp.exp(mst[b, 0:1, :] - lse)
        d_b = jnp.where(diag, both[0:128] * coef, 0.0).astype(BF16)
        dbd[b, 0:128, :] = d_b
        delta = jnp.sum(d_b.astype(F32) * both[128:256], axis=0, keepdims=True)
        dbd[b, 128:144, :] = pick_row(row16, [-x for x in split3(delta)]).astype(BF16)

    def backward_block(l, c, fresh):
        b = FIRST[l] + c
        prob = probs[b]
        d_prob = nn(kvo[l, :, 128:384], dbd[b])
        d_score = prob * d_prob.astype(BF16)
        d_q = nn(kvt[l, 0:128, :], d_score) * 0.125
        d_k = nt(d_score, qbd[b])
        d_v = nt(prob, dbd[b, 0:128, :])
        if fresh:
            dkv[:, 0:128] = d_k
            dkv[:, 128:256] = d_v
        else:
            dkv[:, 0:128] += d_k
            dkv[:, 128:256] += d_v
        if l == 0:
            where = pl.ds(pl.multiple_of(c * C, C), C)
            qacc[where, :] += jnp.where(top, d_q[:, :C], d_q[:, C:]).T
        else:
            tok = C << l
            placed = nt(sels[l][...], jnp.where(diag, d_q, 0.0).astype(BF16))
            if l == 3:
                qacc[...] = placed
            else:
                qacc[pl.ds(pl.multiple_of(c * tok, tok), tok), :] += placed

    def g_copy(l, d):
        n = T >> l
        i = slot(l, d)
        part = lax.rem(rank[l] + d, 1 << l)
        return pltpu.make_async_remote_copy(
            src_ref=gsend[l].at[pl.ds(pl.multiple_of(part * n, n), n), :],
            dst_ref=grecv[l].at[d - 1],
            send_sem=gr_ss.at[i],
            recv_sem=gr_rs.at[i],
            device_id=(member(l, d), hx),
            device_id_type=MESH,
        )

    for l in (3, 2, 1, 0):
        for c in range(COUNT[l]):
            prepare(l, c)
        backward_block(l, 0, True)
        if COUNT[l] > 1:
            pl.loop(1, COUNT[l])(lambda c: backward_block(l, c, False))
        if l:
            n = T >> l
            gsend[l][...] = dkv[...].astype(BF16)
            for d in range(1, 1 << l):
                g_copy(l, d).start()
            owns[l][...] = dkv[pl.ds(pl.multiple_of(rank[l] * n, n), n), :]

    dq_ref[...] = qacc[...].astype(BF16)

    for d in range(1, nh):
        a_copy(d).wait_recv()
    layer_ref[...] = nn(att[...], wfull[...]).astype(BF16)

    for l in (3, 2, 1):
        tok = C << l
        for d in range(1, 1 << l):
            g_copy(l, d).wait_recv()
        for c in range(COUNT[l]):
            rows = slice(c * C, (c + 1) * C)
            grad = owns[l][rows, :]
            for d in range(1, 1 << l):
                grad = grad + grecv[l][d - 1, rows, :].astype(F32)
            stacked = jnp.concatenate(
                [jnp.where(kv_head1, 0.0, grad), jnp.where(kv_head1, grad, 0.0)], axis=0
            ).astype(BF16)
            dkv[c * tok : (c + 1) * tok, :] += nn(sels[l][...], stacked)
    dk_ref[...] = dkv[:, 0:128].astype(BF16)
    dv_ref[...] = dkv[:, 128:256].astype(BF16)

    for d in range(1, nh):
        w_copy(d).wait_send()
        d_copy(d).wait_send()
        a_copy(d).wait_send()
    for l in (1, 2, 3):
        for d in range(1, 1 << l):
            kv_copy(l, d).wait_send()
            g_copy(l, d).wait_send()


def shards(nh, queries, key_rows, value_rows, offsets, w_out, d_out):
    vmem = pl.BlockSpec(memory_space=pltpu.VMEM)
    dma = pltpu.SemaphoreType.DMA
    feat = 128 * nh
    level_bf16 = [pltpu.VMEM((T >> l, 256), BF16) for l in (1, 2, 3)]
    scratch = [
        *[pltpu.VMEM((C << l, 256), BF16) for l in (1, 2, 3)],
        pltpu.VMEM((128, T), BF16),
        pltpu.VMEM((LEVELS, T, 384), BF16),
        pltpu.VMEM((LEVELS, 272, T), BF16),
        pltpu.VMEM((BLOCKS, 128, 256), BF16),
        pltpu.VMEM((BLOCKS, 256, 256), BF16),
        pltpu.VMEM((BLOCKS, T, 256), BF16),
        pltpu.VMEM((BLOCKS, 8, 256), F32),
        *level_bf16,
        pltpu.VMEM((feat, 256), BF16),
        pltpu.VMEM((feat, T), BF16),
        pltpu.VMEM((max(nh - 1, 1), 128, T), BF16),
        pltpu.VMEM((272, T), BF16),
        pltpu.VMEM((LEVELS, 128, T), F32),
        pltpu.VMEM((LEVELS, 8, T), F32),
        pltpu.VMEM((T, feat), BF16),
        pltpu.VMEM((T, 128), F32),
        pltpu.VMEM((T, 256), F32),
        *[pltpu.VMEM((T, 256), BF16) for l in (1, 2, 3)],
        *[pltpu.VMEM(((1 << l) - 1, T >> l, 256), BF16) for l in (1, 2, 3)],
        *[pltpu.VMEM((T >> l, 256), F32) for l in (1, 2, 3)],
        dma((11,)),
        dma((11,)),
        dma((11,)),
        dma((11,)),
        *[dma((max(nh - 1, 1),))] * 6,
    ]
    return pl.pallas_call(
        functools.partial(kernel, nh),
        out_shape=(
            jax.ShapeDtypeStruct((T, 256), BF16),
            jax.ShapeDtypeStruct((T, 128), BF16),
            jax.ShapeDtypeStruct((T, 128), BF16),
            jax.ShapeDtypeStruct((T, 128), BF16),
        ),
        in_specs=[pl.BlockSpec(memory_space=pltpu.SMEM)] + [vmem] * 5,
        out_specs=(vmem,) * 4,
        scratch_shapes=scratch,
        compiler_params=pltpu.CompilerParams(
            collective_id=0, has_side_effects=True, vmem_limit_bytes=56 * 1024 * 1024
        ),
        cost_estimate=pl.CostEstimate(flops=4_000_000_000, bytes_accessed=3_000_000, transcendentals=4_000_000),
    )(offsets, queries, key_rows, value_rows, w_out, d_out)


def solution(mesh):
    in_specs = (
        P("seq", "head"),
        P("seq", "head"),
        P("seq", "head"),
        P(None, "head"),
        P("head", None),
        P("seq", "head"),
    )
    out_specs = (P("seq", "head"), P("seq", "head"), P("seq", "head"), P("seq", "head"))
    return jax.shard_map(
        functools.partial(shards, mesh.shape["head"]),
        mesh=mesh,
        in_specs=in_specs,
        out_specs=out_specs,
        check_vma=False,
    )
```

profile of v0, /device:TPU:1, one launch (start us, length us, event | category | flops | bytes accessed | tf_op | source)
XLA Modules:
  0.0 51.4 jit_solution(6721637343510679081)
XLA Ops:
  0.6 1.3 %copy.10.off = s32[4,2]{1,0:T(4,128)} copy(s32[4,2]{0,1:T(2,128)} %param.9) | data formatting | bytes 64 | tf_op args[3]
  2.0 44.7 %shard_map.93 = (bf16[1024,256]{1,0:T(8,128)(2,1)}, bf16[1024,128]{1,0:T(8,128)(2,1)}, bf16[1024,128]{1,0:T(8,128)(2,1)}, bf16[1024,128]{1,0:T(8,128)(2,1)}) custom-call(s32[4,2]{1,0:T(4,128)} %copy.10.off, bf16[1024,128]{1,0:T(8,128)(2,1)} %q_ref.1, bf16[1024,128]{1,0:T(8,128)(2,1)} %k_ref.1, bf16[1024,128]{1,0:T(8,128)(2,1)} %v_ref.1, ...), custom_call_target="tpu_custom_call" | custom-call | flops 4000000000 | bytes 3000000 | tf_op jit(solution)/shard_map/pallas_call | solution.py:435
  46.6 0.0 copy-start.2
  46.7 1.9 %copy.15 = bf16[1024,256]{1,0:T(8,128)(2,1)} copy(bf16[1024,256]{1,0:T(8,128)(2,1)} %get-tuple-element.8) | data formatting | bytes 1048576
  48.6 0.0 copy-done.2
  48.6 0.0 copy-start.1
  48.6 0.7 %copy.16 = bf16[1024,128]{1,0:T(8,128)(2,1)} copy(bf16[1024,128]{1,0:T(8,128)(2,1)S(1)} %copy-done.2) | data formatting | bytes 524288
  49.3 0.3 copy-done.1
  49.6 0.0 copy-start
  49.6 0.7 %copy.17 = bf16[1024,128]{1,0:T(8,128)(2,1)} copy(bf16[1024,128]{1,0:T(8,128)(2,1)S(1)} %copy-done.1) | data formatting | bytes 524288
  50.3 0.3 copy-done
  50.7 0.7 %copy.18 = bf16[1024,128]{1,0:T(8,128)(2,1)} copy(bf16[1024,128]{1,0:T(8,128)(2,1)S(1)} %copy-done) | data formatting | bytes 524288
Async XLA Ops:
  46.6 1.9 %copy-start.2 = (bf16[1024,128]{1,0:T(8,128)(2,1)S(1)}, bf16[1024,128]{1,0:T(8,128)(2,1)}, u32[]{:S(2)}) copy-start(bf16[1024,128]{1,0:T(8,128)(2,1)} %get-tuple-element.9) | copy-start | bytes 786436
  48.6 1.0 %copy-start.1 = (bf16[1024,128]{1,0:T(8,128)(2,1)S(1)}, bf16[1024,128]{1,0:T(8,128)(2,1)}, u32[]{:S(2)}) copy-start(bf16[1024,128]{1,0:T(8,128)(2,1)} %get-tuple-element.10) | copy-start | bytes 786436
  49.6 1.0 %copy-start = (bf16[1024,128]{1,0:T(8,128)(2,1)S(1)}, bf16[1024,128]{1,0:T(8,128)(2,1)}, u32[]{:S(2)}) copy-start(bf16[1024,128]{1,0:T(8,128)(2,1)} %get-tuple-element.11) | copy-start | bytes 786436
where the time goes:
time: 51.6 us; the launch traced here: 51.4 us
  Pallas kernels  44.7 us (87%)
  local copies, waits for them, and re-layouts  6.04 us (12%)
  between operations  0.65 us (1%)
    pallas_call x1, Pallas kernels, shards(): pl.pallas_call(functools.partial(kernel, nh), out_shape=(jax.ShapeDtypeSt...  44.7 us
    unnamed x11, local copies, waits for them, and re-layouts  6.04 us

commit v1 on v0

v1 whole, which is shorter than its diff:
```python
import functools

import jax
import jax.numpy as jnp
from jax import lax
from jax.experimental import pallas as pl
from jax.experimental.pallas import tpu as pltpu
from jax.sharding import PartitionSpec as P

MESH = pl.DeviceIdType.MESH
HD = 64
LEVELS = 4
T = 1024
C = 128
FIRST = (0, 8, 12, 14)
COUNT = (8, 4, 2, 1)
BLOCKS = 15
F32, BF16 = jnp.float32, jnp.bfloat16


def nn(a, b):
    return lax.dot_general(a, b, (((1,), (0,)), ((), ())), preferred_element_type=F32)


def nt(a, b):
    return lax.dot_general(a, b, (((1,), (1,)), ((), ())), preferred_element_type=F32)


def iota(shape, dim):
    return lax.broadcasted_iota(jnp.int32, shape, dim)


def split3(x):
    hi = x.astype(BF16)
    rest = x - hi.astype(F32)
    mid = rest.astype(BF16)
    lo = (rest - mid.astype(F32)).astype(BF16)
    return hi.astype(F32), mid.astype(F32), lo.astype(F32)


def pick_row(row, values):
    out = jnp.zeros_like(values[0] + row.astype(F32))
    for i, value in enumerate(values):
        out = jnp.where(row == i, value, out)
    return out


def kernel(
    nh,
    off,
    q_ref,
    k_ref,
    v_ref,
    w_ref,
    g_ref,
    layer_ref,
    dq_ref,
    dk_ref,
    dv_ref,
    sel1,
    sel2,
    sel3,
    qt,
    kv1,
    kv2,
    kv3,
    kvt,
    qbd,
    dbd,
    probs,
    grads,
    scores,
    kvs1,
    kvs2,
    kvs3,
    wfull,
    dsend,
    drecv,
    dap,
    toko,
    tokl,
    att,
    dkv,
    dqs,
    gs1,
    gs2,
    gs3,
    gr1,
    gr2,
    gr3,
    own1,
    own2,
    own3,
    stk1,
    stk2,
    stk3,
    kv_ss,
    kv_rs,
    gr_ss,
    gr_rs,
    w_ss,
    w_rs,
    d_ss,
    d_rs,
    a_ss,
    a_rs,
):
    sels = (None, sel1, sel2, sel3)
    kvs = (None, kvs1, kvs2, kvs3)
    kv = (None, kv1, kv2, kv3)
    gsend = (None, gs1, gs2, gs3)
    grecv = (None, gr1, gr2, gr3)
    owns = (None, own1, own2, own3)
    stacks = (None, stk1, stk2, stk3)
    seq = lax.axis_index("seq")
    hx = lax.axis_index("head")
    rank = [lax.rem(seq, 1 << l) for l in range(LEVELS)]

    def member(l, d):
        return seq - rank[l] + lax.rem(rank[l] + d, 1 << l)

    def slot(l, d):
        return (1 << l) - 2 - l + d if l else 0

    def head_peer(d):
        return lax.rem(hx + d, nh)

    def keys(l):
        return k_ref[...] if l == 0 else kv[l][:, 0:128]

    def values(l):
        return v_ref[...] if l == 0 else kv[l][:, 128:256]

    barrier = pltpu.get_barrier_semaphore()
    for d in range(1, 8):
        pl.semaphore_signal(barrier, inc=1, device_id=(member(3, d), hx), device_id_type=MESH)
    for d in range(1, nh):
        pl.semaphore_signal(barrier, inc=1, device_id=(seq, head_peer(d)), device_id_type=MESH)
    pl.semaphore_wait(barrier, 7 + nh - 1)

    own_rows = pl.ds(pl.multiple_of(hx * 128, 128), 128)

    def w_copy(d):
        return pltpu.make_async_remote_copy(
            src_ref=w_ref.at[:, pl.ds(pl.multiple_of(head_peer(d) * 256, 256), 256)],
            dst_ref=wfull.at[own_rows, :],
            send_sem=w_ss.at[d - 1],
            recv_sem=w_rs.at[d - 1],
            device_id=(seq, head_peer(d)),
            device_id_type=MESH,
        )

    for d in range(1, nh):
        w_copy(d).start()
    wfull[own_rows, :] = w_ref[:, pl.ds(pl.multiple_of(hx * 256, 256), 256)]

    lane = iota((1, 256), 1)
    second = lane >= C
    offs = [[lax.rem(off[l, h], 1 << l) for h in range(2)] for l in range(LEVELS)]

    def kv_copy(l, d):
        n = T >> l
        i = slot(l, d)
        return pltpu.make_async_remote_copy(
            src_ref=kvs[l],
            dst_ref=kv[l].at[pl.ds(pl.multiple_of(rank[l] * n, n), n), :],
            send_sem=kv_ss.at[i],
            recv_sem=kv_rs.at[i],
            device_id=(member(l, d), hx),
            device_id_type=MESH,
        )

    kv_head1 = lax.rem(iota((C, 256), 1), 128) >= HD
    for l in (3, 2, 1):
        r = 1 << l
        tok = C * r
        n = T >> l
        row2 = iota((256, tok), 0)
        target = lax.rem(row2, C) * r + jnp.where(row2 >= C, offs[l][1], offs[l][0])
        selt = jnp.where(iota((256, tok), 1) == target, 1.0, 0.0).astype(BF16)
        for c in range(COUNT[l]):
            rows = slice(c * tok, (c + 1) * tok)
            both = nn(selt, jnp.concatenate([k_ref[rows, :], v_ref[rows, :]], axis=1))
            kvs[l][c * C : (c + 1) * C, :] = jnp.where(kv_head1, both[C:], both[:C]).astype(BF16)
        for d in range(1, r):
            kv_copy(l, d).start()
        kv[l][pl.ds(pl.multiple_of(rank[l] * n, n), n), :] = kvs[l][...]

    eye = jnp.where(iota((256, 256), 0) == iota((256, 256), 1), 1.0, 0.0).astype(BF16)
    diag = (iota((C, 256), 0) >= HD) == (iota((C, 256), 1) >= C)
    row16 = iota((16, 256), 0)
    own_row = lax.div(row16, 3) == lax.div(iota((16, 256), 1), C)
    top = iota((C, C), 0) < HD
    ones16 = jnp.ones((16, T), BF16)
    ones128 = jnp.ones((T, 128), BF16)
    zeros112 = jnp.zeros((112, 256), BF16)

    qt[...] = (nt(eye[:C, :C], q_ref[...]) * 0.125).astype(BF16)

    def place_queries(l):
        tok = C << l
        if l:
            target = lax.rem(lane, C) * (1 << l) + jnp.where(second, offs[l][1], offs[l][0])
            sels[l][...] = jnp.where(iota((tok, 256), 0) == target, 1.0, 0.0).astype(BF16)
        for c in range(COUNT[l]):
            part = qt[:, c * tok : (c + 1) * tok]
            if l == 0:
                both = jnp.concatenate([part, part], axis=1).astype(F32)
            else:
                both = nn(part, sels[l][...])
            qbd[FIRST[l] + c] = jnp.where(diag, both, 0.0).astype(BF16)

    def transpose_kv(l):
        for c in range(4):
            rows = slice(c * 256, (c + 1) * 256)
            if l == 0:
                part = jnp.concatenate([k_ref[rows, :], v_ref[rows, :]], axis=1)
            else:
                part = kv[l][rows, :]
            kvt[l, :, rows] = nt(eye, part).astype(BF16)

    where = [(l, c) for l in range(LEVELS) for c in range(COUNT[l])]
    top_scores = {}

    def score_stage(b):
        l, c = where[b]
        score = nn(keys(l), qbd[b])
        scores[b % 2] = score
        top_scores[b] = jnp.max(score, axis=0, keepdims=True)

    def prob_stage(b):
        probs[b] = jnp.exp(scores[b % 2] - top_scores[b]).astype(BF16)

    def out_stage(b):
        l, c = where[b]
        out = nn(jnp.concatenate([kvt[l, 128:256, :], ones16], axis=0), probs[b])
        total = out[C : C + 1]
        lse = top_scores[b] + jnp.log(total)
        out = out[:C] * (1.0 / total)
        if l == 0:
            cols = slice(c * C, (c + 1) * C)
            toko[0, :, cols] = jnp.where(top, out[:, :C], out[:, C:])
            tokl[0, 0:1, cols] = lse[:, :C]
            tokl[0, 1:2, cols] = lse[:, C:]
            return
        r = 1 << l
        tok = C * r
        cols = slice(c * tok, (c + 1) * tok)
        pieces = pick_row(lax.rem(row16, 3), split3(lse))
        pieces = jnp.where(own_row, pieces, 0.0)
        packed = jnp.concatenate([jnp.where(diag, out, 0.0), pieces], axis=0).astype(BF16)
        placed = nt(packed, sels[l][...])
        toko[l, :, cols] = placed[:C]
        phase = lax.rem(iota((1, tok), 1), r)
        for h in range(2):
            i = C + 3 * h
            value = placed[i : i + 1] + placed[i + 1 : i + 2] + placed[i + 2 : i + 3]
            tokl[l, h : h + 1, cols] = jnp.where(phase == offs[l][h], value, -1e30)

    def d_copy(d):
        return pltpu.make_async_remote_copy(
            src_ref=dsend.at[pl.ds(pl.multiple_of(head_peer(d) * 128, 128), 128), :],
            dst_ref=drecv.at[d - 1],
            send_sem=d_ss.at[d - 1],
            recv_sem=d_rs.at[d - 1],
            device_id=(seq, head_peer(d)),
            device_id_type=MESH,
        )

    place_queries(0)
    for step in range(BLOCKS + 2):
        if step == 4:
            for d in range(1, nh):
                w_copy(d).wait_recv()
            for c in range(4):
                cols = slice(c * 256, (c + 1) * 256)
                dsend[:, cols] = nt(wfull[...], g_ref[cols, :]).astype(BF16)
            for d in range(1, nh):
                d_copy(d).start()
        if step in FIRST[1:]:
            l = FIRST.index(step)
            for d in range(1, 1 << l):
                kv_copy(l, d).wait_recv()
            transpose_kv(l)
        if step < BLOCKS:
            score_stage(step)
        if step == 0:
            transpose_kv(0)
        if step in (1, 2, 3):
            place_queries(step)
        if 0 <= step - 1 < BLOCKS:
            prob_stage(step - 1)
        if 0 <= step - 2:
            out_stage(step - 2)

    lses = [tokl[l, 0:2, :] for l in range(LEVELS)]
    peak = jnp.maximum(jnp.maximum(lses[0], lses[1]), jnp.maximum(lses[2], lses[3]))
    total = sum(jnp.exp(x - peak) for x in lses)
    joint = peak + jnp.log(total)
    is_top = iota((C, T), 0) < HD
    mixed = jnp.zeros((C, T), F32)
    for l in range(LEVELS):
        weight = jnp.exp(lses[l] - joint)
        mixed = mixed + jnp.where(is_top, weight[0:1], weight[1:2]) * toko[l]
    mixed_b = mixed.astype(BF16)
    dap[128:256, :] = mixed_b
    att[:, own_rows] = mixed_b.astype(F32).T.astype(BF16)

    def a_copy(d):
        return pltpu.make_async_remote_copy(
            src_ref=att.at[:, own_rows],
            dst_ref=att.at[:, own_rows],
            send_sem=a_ss.at[d - 1],
            recv_sem=a_rs.at[d - 1],
            device_id=(seq, head_peer(d)),
            device_id_type=MESH,
        )

    for d in range(1, nh):
        a_copy(d).start()

    rowt = iota((16, T), 0)
    hi, mid, lo = split3(joint)
    dap[256:272, :] = pick_row(
        rowt, (hi[0:1], mid[0:1], lo[0:1], hi[1:2], mid[1:2], lo[1:2])
    ).astype(BF16)

    for d in range(1, nh):
        d_copy(d).wait_recv()
    d_sum = dsend[own_rows, :].astype(F32)
    for d in range(1, nh):
        d_sum = d_sum + drecv[d - 1].astype(F32)
    dap[0:128, :] = d_sum.astype(BF16)

    def prepare(b):
        l, c = where[b]
        tok = C << l
        part = dap[:, c * tok : (c + 1) * tok]
        if l == 0:
            both = jnp.concatenate([part, part], axis=1).astype(F32)
        else:
            both = nn(part, sels[l][...])
        x = both[256:272]
        lse = jnp.where(second, x[3:4] + x[4:5] + x[5:6], x[0:1] + x[1:2] + x[2:3])
        coef = jnp.exp(top_scores[b] - lse)
        d_b = jnp.where(diag, both[0:128] * coef, 0.0).astype(BF16)
        dbd[b, 0:128, :] = d_b
        delta = jnp.sum(d_b.astype(F32) * both[128:256], axis=0, keepdims=True)
        dbd[b, 128:144, :] = pick_row(row16, [-x for x in split3(delta)]).astype(BF16)

    def grad_stage(b):
        l, c = where[b]
        d_prob = nn(
            jnp.concatenate([values(l), ones128], axis=1),
            jnp.concatenate([dbd[b], zeros112], axis=0),
        )
        grads[b] = probs[b] * d_prob.astype(BF16)

    def query_stage(b):
        l, c = where[b]
        d_q = nn(kvt[l, 0:128, :], grads[b]) * 0.125
        if l == 0:
            dqs[b] = jnp.where(top, d_q[:, :C], d_q[:, C:]).T
        else:
            qbd[b] = jnp.where(diag, d_q, 0.0).astype(BF16)

    def side(refs):
        return jnp.concatenate(refs, axis=1)

    def key_stage(blocks, fresh):
        d_k = nt(side([grads[b] for b in blocks]), side([qbd[b] for b in blocks]))
        d_v = nt(side([probs[b] for b in blocks]), side([dbd[b, 0:128, :] for b in blocks]))
        if fresh:
            dkv[:, 0:128] = d_k
            dkv[:, 128:256] = d_v
        else:
            dkv[:, 0:128] += d_k
            dkv[:, 128:256] += d_v

    def g_copy(l, d):
        n = T >> l
        i = slot(l, d)
        part = lax.rem(rank[l] + d, 1 << l)
        return pltpu.make_async_remote_copy(
            src_ref=gsend[l].at[pl.ds(pl.multiple_of(part * n, n), n), :],
            dst_ref=grecv[l].at[d - 1],
            send_sem=gr_ss.at[i],
            recv_sem=gr_rs.at[i],
            device_id=(member(l, d), hx),
            device_id_type=MESH,
        )

    groups = [[14], [12, 13], [8, 9, 10, 11], [0, 1, 2, 3], [4, 5, 6, 7]]
    for b in groups[0]:
        prepare(b)
        grad_stage(b)
    for i, group in enumerate(groups):
        if i + 1 < len(groups):
            for b in groups[i + 1]:
                prepare(b)
                grad_stage(b)
        key_stage(group, group[0] != 4)
        for b in group:
            query_stage(b)
        l = where[group[0]][0]
        if l:
            n = T >> l
            gsend[l][...] = dkv[...].astype(BF16)
            for d in range(1, 1 << l):
                g_copy(l, d).start()
            owns[l][...] = dkv[pl.ds(pl.multiple_of(rank[l] * n, n), n), :]

    for d in range(1, nh):
        a_copy(d).wait_recv()
    layer_ref[...] = nn(att[...], wfull[...]).astype(BF16)

    for l in (3, 2, 1):
        for d in range(1, 1 << l):
            g_copy(l, d).wait_recv()
    for l in (3, 2, 1):
        for c in range(COUNT[l]):
            rows = slice(c * C, (c + 1) * C)
            grad = owns[l][rows, :]
            for d in range(1, 1 << l):
                grad = grad + grecv[l][d - 1, rows, :].astype(F32)
            stacks[l][c, 0:C, :] = jnp.where(kv_head1, 0.0, grad).astype(BF16)
            stacks[l][c, C:256, :] = jnp.where(kv_head1, grad, 0.0).astype(BF16)
    for c in range(4):
        rows = slice(c * 256, (c + 1) * 256)
        place = side([sel1[...], sel2[c % 2 * 256 : c % 2 * 256 + 256, :], sel3[rows, :]])
        d_q = nt(place, side([qbd[8 + c], qbd[12 + c // 2], qbd[14]]))
        for half in range(2):
            part = slice(half * C, half * C + C)
            d_rows = slice(c * 256 + half * C, c * 256 + half * C + C)
            dq_ref[d_rows, :] = (d_q[part] + dqs[2 * c + half]).astype(BF16)
        d_kv = dkv[rows, :] + nn(
            place, jnp.concatenate([stk1[c], stk2[c // 2], stk3[0]], axis=0)
        )
        dk_ref[rows, :] = d_kv[:, 0:128].astype(BF16)
        dv_ref[rows, :] = d_kv[:, 128:256].astype(BF16)

    for d in range(1, nh):
        w_copy(d).wait_send()
        d_copy(d).wait_send()
        a_copy(d).wait_send()
    for l in (1, 2, 3):
        for d in range(1, 1 << l):
            kv_copy(l, d).wait_send()
            g_copy(l, d).wait_send()


def shards(nh, queries, key_rows, value_rows, offsets, w_out, d_out):
    vmem = pl.BlockSpec(memory_space=pltpu.VMEM)
    dma = pltpu.SemaphoreType.DMA
    feat = 128 * nh
    scratch = [
        *[pltpu.VMEM((C << l, 256), BF16) for l in (1, 2, 3)],
        pltpu.VMEM((128, T), BF16),
        *[pltpu.VMEM((T, 256), BF16) for l in (1, 2, 3)],
        pltpu.VMEM((LEVELS, 256, T), BF16),
        pltpu.VMEM((BLOCKS, 128, 256), BF16),
        pltpu.VMEM((BLOCKS, 144, 256), BF16),
        pltpu.VMEM((BLOCKS, T, 256), BF16),
        pltpu.VMEM((BLOCKS, T, 256), BF16),
        pltpu.VMEM((2, T, 256), F32),
        *[pltpu.VMEM((T >> l, 256), BF16) for l in (1, 2, 3)],
        pltpu.VMEM((feat, 256), BF16),
        pltpu.VMEM((feat, T), BF16),
        pltpu.VMEM((max(nh - 1, 1), 128, T), BF16),
        pltpu.VMEM((272, T), BF16),
        pltpu.VMEM((LEVELS, 128, T), F32),
        pltpu.VMEM((LEVELS, 8, T), F32),
        pltpu.VMEM((T, feat), BF16),
        pltpu.VMEM((T, 256), F32),
        pltpu.VMEM((8, C, 128), F32),
        *[pltpu.VMEM((T, 256), BF16) for l in (1, 2, 3)],
        *[pltpu.VMEM(((1 << l) - 1, T >> l, 256), BF16) for l in (1, 2, 3)],
        *[pltpu.VMEM((T >> l, 256), F32) for l in (1, 2, 3)],
        *[pltpu.VMEM((COUNT[l], 256, 256), BF16) for l in (1, 2, 3)],
        dma((11,)),
        dma((11,)),
        dma((11,)),
        dma((11,)),
        *[dma((max(nh - 1, 1),))] * 6,
    ]
    return pl.pallas_call(
        functools.partial(kernel, nh),
        out_shape=(
            jax.ShapeDtypeStruct((T, 256), BF16),
            jax.ShapeDtypeStruct((T, 128), BF16),
            jax.ShapeDtypeStruct((T, 128), BF16),
            jax.ShapeDtypeStruct((T, 128), BF16),
        ),
        in_specs=[pl.BlockSpec(memory_space=pltpu.SMEM)] + [vmem] * 5,
        out_specs=(vmem,) * 4,
        scratch_shapes=scratch,
        compiler_params=pltpu.CompilerParams(
            collective_id=0, has_side_effects=True, vmem_limit_bytes=56 * 1024 * 1024
        ),
        cost_estimate=pl.CostEstimate(flops=4_000_000_000, bytes_accessed=3_000_000, transcendentals=4_000_000),
    )(offsets, queries, key_rows, value_rows, w_out, d_out)


def solution(mesh):
    in_specs = (
        P("seq", "head"),
        P("seq", "head"),
        P("seq", "head"),
        P(None, "head"),
        P("head", None),
        P("seq", "head"),
    )
    out_specs = (P("seq", "head"), P("seq", "head"), P("seq", "head"), P("seq", "head"))
    return jax.shard_map(
        functools.partial(shards, mesh.shape["head"]),
        mesh=mesh,
        in_specs=in_specs,
        out_specs=out_specs,
        check_vma=False,
    )
```

time: 51.6 us -> 49.4 us (0.957)
  Pallas kernels: 44.7 us -> 42.5 us
    pallas_call x1, Pallas kernels: 44.7 us -> 42.5 us  [shards(): pl.pallas_call(functools.partial(kernel, nh), out_shape=(jax.ShapeDtypeSt...]
where the time goes in v1:
time: 49.4 us; the launch traced here: 49.2 us
  Pallas kernels  42.5 us (86%)
  local copies, waits for them, and re-layouts  6.04 us (12%)
  between operations  0.65 us (1%)
    pallas_call x1, Pallas kernels, shards(): pl.pallas_call(functools.partial(kernel, nh), out_shape=(jax.ShapeDtypeSt...  42.5 us
    unnamed x11, local copies, waits for them, and re-layouts  6.04 us

profile of v1, /device:TPU:1, one launch (start us, length us, event | category | flops | bytes accessed | tf_op | source)
XLA Modules:
  0.0 49.2 jit_solution(5163040683246001150)
XLA Ops:
  0.6 1.3 %copy.10.off = s32[4,2]{1,0:T(4,128)} copy(s32[4,2]{0,1:T(2,128)} %param.9) | data formatting | bytes 64 | tf_op args[3]
  2.0 42.5 %shard_map.93 = (bf16[1024,256]{1,0:T(8,128)(2,1)}, bf16[1024,128]{1,0:T(8,128)(2,1)}, bf16[1024,128]{1,0:T(8,128)(2,1)}, bf16[1024,128]{1,0:T(8,128)(2,1)}) custom-call(s32[4,2]{1,0:T(4,128)} %copy.10.off, bf16[1024,128]{1,0:T(8,128)(2,1)} %q_ref.1, bf16[1024,128]{1,0:T(8,128)(2,1)} %k_ref.1, bf16[1024,128]{1,0:T(8,128)(2,1)} %v_ref.1, ...), custom_call_target="tpu_custom_call" | custom-call | flops 4000000000 | bytes 3000000 | tf_op jit(solution)/shard_map/pallas_call | solution.py:486
  44.4 0.0 copy-start.2
  44.5 1.9 %copy.15 = bf16[1024,256]{1,0:T(8,128)(2,1)} copy(bf16[1024,256]{1,0:T(8,128)(2,1)} %get-tuple-element.8) | data formatting | bytes 1048576
  46.4 0.0 copy-done.2
  46.4 0.0 copy-start.1
  46.4 0.7 %copy.16 = bf16[1024,128]{1,0:T(8,128)(2,1)} copy(bf16[1024,128]{1,0:T(8,128)(2,1)S(1)} %copy-done.2) | data formatting | bytes 524288
  47.1 0.3 copy-done.1
  47.4 0.0 copy-start
  47.4 0.7 %copy.17 = bf16[1024,128]{1,0:T(8,128)(2,1)} copy(bf16[1024,128]{1,0:T(8,128)(2,1)S(1)} %copy-done.1) | data formatting | bytes 524288
  48.1 0.3 copy-done
  48.5 0.7 %copy.18 = bf16[1024,128]{1,0:T(8,128)(2,1)} copy(bf16[1024,128]{1,0:T(8,128)(2,1)S(1)} %copy-done) | data formatting | bytes 524288
Async XLA Ops:
  44.4 1.9 %copy-start.2 = (bf16[1024,128]{1,0:T(8,128)(2,1)S(1)}, bf16[1024,128]{1,0:T(8,128)(2,1)}, u32[]{:S(2)}) copy-start(bf16[1024,128]{1,0:T(8,128)(2,1)} %get-tuple-element.9) | copy-start | bytes 786436
  46.4 1.0 %copy-start.1 = (bf16[1024,128]{1,0:T(8,128)(2,1)S(1)}, bf16[1024,128]{1,0:T(8,128)(2,1)}, u32[]{:S(2)}) copy-start(bf16[1024,128]{1,0:T(8,128)(2,1)} %get-tuple-element.10) | copy-start | bytes 786436
  47.4 1.0 %copy-start = (bf16[1024,128]{1,0:T(8,128)(2,1)S(1)}, bf16[1024,128]{1,0:T(8,128)(2,1)}, u32[]{:S(2)}) copy-start(bf16[1024,128]{1,0:T(8,128)(2,1)} %get-tuple-element.11) | copy-start | bytes 786436

commit v2 on v1

--- a/solution.py
+++ b/solution.py
@@ -16,6 +16,9 @@
 COUNT = (8, 4, 2, 1)
 BLOCKS = 15
 F32, BF16 = jnp.float32, jnp.bfloat16
+W_STEP = 4
+D_STEP = 11
+PASS_STEP = (0, 0, 7, 9)
 
 
 def nn(a, b):
@@ -48,15 +51,20 @@
 def kernel(
     nh,
     off,
+    q_hbm,
+    k_hbm,
+    v_hbm,
+    w_hbm,
+    g_hbm,
+    layer_ref,
+    dq_ref,
+    dk_ref,
+    dv_ref,
     q_ref,
     k_ref,
     v_ref,
     w_ref,
     g_ref,
-    layer_ref,
-    dq_ref,
-    dk_ref,
-    dv_ref,
     sel1,
     sel2,
     sel3,
@@ -75,6 +83,8 @@
     kvs3,
     wfull,
     dsend,
+    dpass,
+    dsum,
     drecv,
     dap,
     toko,
@@ -85,12 +95,14 @@
     gs1,
     gs2,
     gs3,
+    gx2,
+    gx3,
+    gt2,
+    gt3,
     gr1,
     gr2,
     gr3,
     own1,
-    own2,
-    own3,
     stk1,
     stk2,
     stk3,
@@ -104,27 +116,48 @@
     d_rs,
     a_ss,
     a_rs,
+    in_sem,
 ):
     sels = (None, sel1, sel2, sel3)
     kvs = (None, kvs1, kvs2, kvs3)
     kv = (None, kv1, kv2, kv3)
     gsend = (None, gs1, gs2, gs3)
+    gother = (None, None, gx2, gx3)
+    gtotal = (None, None, gt2, gt3)
     grecv = (None, gr1, gr2, gr3)
-    owns = (None, own1, own2, own3)
     stacks = (None, stk1, stk2, stk3)
     seq = lax.axis_index("seq")
     hx = lax.axis_index("head")
     rank = [lax.rem(seq, 1 << l) for l in range(LEVELS)]
-
-    def member(l, d):
-        return seq - rank[l] + lax.rem(rank[l] + d, 1 << l)
-
-    def slot(l, d):
-        return (1 << l) - 2 - l + d if l else 0
+    core = rank[1]
+    y = lax.div(rank[3], 2)
+    right, left = lax.rem(hx + 1, nh), lax.rem(hx + nh - 1, nh)
+    sibling = (seq + 1 - 2 * core, hx)
+
+    def column(l, dy):
+        span = 1 << (l - 1)
+        at = lax.rem(y, span)
+        return y - at + lax.rem(at + dy, span)
+
+    def along(y_to):
+        return (seq - rank[3] + y_to * 2 + core, hx)
 
     def head_peer(d):
         return lax.rem(hx + d, nh)
 
+    def remote(src, dst, sems, i, device):
+        return pltpu.make_async_remote_copy(
+            src_ref=src,
+            dst_ref=dst,
+            send_sem=sems[0].at[i],
+            recv_sem=sems[1].at[i],
+            device_id=device,
+            device_id_type=MESH,
+        )
+
+    def block(index, size):
+        return pl.ds(pl.multiple_of(index * size, size), size)
+
     def keys(l):
         return k_ref[...] if l == 0 else kv[l][:, 0:128]
 
@@ -132,43 +165,59 @@
         return v_ref[...] if l == 0 else kv[l][:, 128:256]
 
     barrier = pltpu.get_barrier_semaphore()
-    for d in range(1, 8):
-        pl.semaphore_signal(barrier, inc=1, device_id=(member(3, d), hx), device_id_type=MESH)
-    for d in range(1, nh):
-        pl.semaphore_signal(barrier, inc=1, device_id=(seq, head_peer(d)), device_id_type=MESH)
-    pl.semaphore_wait(barrier, 7 + nh - 1)
-
-    own_rows = pl.ds(pl.multiple_of(hx * 128, 128), 128)
+    peers = [sibling] + [along(column(3, dy)) for dy in (1, 2, 3)]
+    peers += [(seq, head_peer(d)) for d in range(1, nh)]
+    for peer in peers:
+        pl.semaphore_signal(barrier, inc=1, device_id=peer, device_id_type=MESH)
+    loads = [
+        pltpu.make_async_copy(src, dst, in_sem.at[i])
+        for i, (src, dst) in enumerate(
+            ((w_hbm, w_ref), (k_hbm, k_ref), (v_hbm, v_ref), (q_hbm, q_ref), (g_hbm, g_ref))
+        )
+    ]
+    for load in loads:
+        load.start()
+    loads[0].wait()
+    pl.semaphore_wait(barrier, len(peers))
+
+    own_rows = block(hx, 128)
 
     def w_copy(d):
-        return pltpu.make_async_remote_copy(
-            src_ref=w_ref.at[:, pl.ds(pl.multiple_of(head_peer(d) * 256, 256), 256)],
-            dst_ref=wfull.at[own_rows, :],
-            send_sem=w_ss.at[d - 1],
-            recv_sem=w_rs.at[d - 1],
-            device_id=(seq, head_peer(d)),
-            device_id_type=MESH,
+        return remote(
+            w_ref.at[:, block(head_peer(d), 256)],
+            wfull.at[own_rows, :],
+            (w_ss, w_rs),
+            d - 1,
+            (seq, head_peer(d)),
         )
 
     for d in range(1, nh):
         w_copy(d).start()
-    wfull[own_rows, :] = w_ref[:, pl.ds(pl.multiple_of(hx * 256, 256), 256)]
+    wfull[own_rows, :] = w_ref[:, block(hx, 256)]
+    loads[1].wait()
+    loads[2].wait()
 
     lane = iota((1, 256), 1)
     second = lane >= C
-    offs = [[lax.rem(off[l, h], 1 << l) for h in range(2)] for l in range(LEVELS)]
-
-    def kv_copy(l, d):
-        n = T >> l
-        i = slot(l, d)
-        return pltpu.make_async_remote_copy(
-            src_ref=kvs[l],
-            dst_ref=kv[l].at[pl.ds(pl.multiple_of(rank[l] * n, n), n), :],
-            send_sem=kv_ss.at[i],
-            recv_sem=kv_rs.at[i],
-            device_id=(member(l, d), hx),
-            device_id_type=MESH,
-        )
+    offs = [[lax.rem(off[h, l], 1 << l) for h in range(2)] for l in range(LEVELS)]
+
+    kv_sems = (kv_ss, kv_rs)
+    kv_base = (0, 0, 1, 4)
+
+    def kv_own(l):
+        return kv[l].at[block(rank[l], T >> l), :]
+
+    def kv_sibling(l):
+        return remote(kvs[l], kv_own(l), kv_sems, kv_base[l], sibling)
+
+    def kv_along(l, dy):
+        return remote(kvs[l], kv_own(l), kv_sems, kv_base[l] + dy, along(column(l, dy)))
+
+    def kv_pass(l, dy):
+        span = 1 << (l - 1)
+        source = column(l, span - dy)
+        part = kv[l].at[block(lax.rem(source, span) * 2 + core, T >> l), :]
+        return remote(part, part, kv_sems, kv_base[l] + span - 1 + dy, sibling)
 
     kv_head1 = lax.rem(iota((C, 256), 1), 128) >= HD
     for l in (3, 2, 1):
@@ -182,9 +231,10 @@
             rows = slice(c * tok, (c + 1) * tok)
             both = nn(selt, jnp.concatenate([k_ref[rows, :], v_ref[rows, :]], axis=1))
             kvs[l][c * C : (c + 1) * C, :] = jnp.where(kv_head1, both[C:], both[:C]).astype(BF16)
-        for d in range(1, r):
-            kv_copy(l, d).start()
-        kv[l][pl.ds(pl.multiple_of(rank[l] * n, n), n), :] = kvs[l][...]
+        for dy in range(1, r // 2):
+            kv_along(l, dy).start()
+        kv_sibling(l).start()
+        kv[l][block(rank[l], n), :] = kvs[l][...]
 
     eye = jnp.where(iota((256, 256), 0) == iota((256, 256), 1), 1.0, 0.0).astype(BF16)
     diag = (iota((C, 256), 0) >= HD) == (iota((C, 256), 1) >= C)
@@ -195,6 +245,8 @@
     ones128 = jnp.ones((T, 128), BF16)
     zeros112 = jnp.zeros((112, 256), BF16)
 
+    loads[3].wait()
+    loads[4].wait()
     qt[...] = (nt(eye[:C, :C], q_ref[...]) * 0.125).astype(BF16)
 
     def place_queries(l):
@@ -257,30 +309,63 @@
             value = placed[i : i + 1] + placed[i + 1 : i + 2] + placed[i + 2 : i + 3]
             tokl[l, h : h + 1, cols] = jnp.where(phase == offs[l][h], value, -1e30)
 
-    def d_copy(d):
-        return pltpu.make_async_remote_copy(
-            src_ref=dsend.at[pl.ds(pl.multiple_of(head_peer(d) * 128, 128), 128), :],
-            dst_ref=drecv.at[d - 1],
-            send_sem=d_ss.at[d - 1],
-            recv_sem=d_rs.at[d - 1],
-            device_id=(seq, head_peer(d)),
-            device_id_type=MESH,
+    d_sems = (d_ss, d_rs)
+    halves = (pl.ds(0, 512), pl.ds(512, 512))
+    sides = (right, left)
+    rows_of = [block(x, 128) for x in sides]
+    opposite = head_peer(2)
+
+    def d_over(i):
+        return remote(
+            dsend.at[block(opposite, 128), halves[i]],
+            dpass.at[i],
+            d_sems,
+            i,
+            (seq, sides[i]),
         )
+
+    def d_plain(i):
+        return remote(
+            dsend.at[rows_of[i], halves[1 - i]],
+            drecv.at[i, :, halves[1 - i]],
+            d_sems,
+            2 + i,
+            (seq, sides[i]),
+        )
+
+    def d_summed(i):
+        return remote(dsum.at[i], drecv.at[i, :, halves[i]], d_sems, 4 + i, (seq, sides[i]))
 
     place_queries(0)
     for step in range(BLOCKS + 2):
-        if step == 4:
+        if step == W_STEP:
             for d in range(1, nh):
                 w_copy(d).wait_recv()
             for c in range(4):
                 cols = slice(c * 256, (c + 1) * 256)
                 dsend[:, cols] = nt(wfull[...], g_ref[cols, :]).astype(BF16)
-            for d in range(1, nh):
-                d_copy(d).start()
+            for i in range(2):
+                d_over(i).start()
+            for i in range(2):
+                d_plain(i).start()
+        if step == D_STEP:
+            for i in range(2):
+                d_over(i).wait_recv()
+            for i in range(2):
+                dsum[i] = (
+                    dsend[rows_of[i], halves[i]].astype(F32) + dpass[i].astype(F32)
+                ).astype(BF16)
+                d_summed(i).start()
+        for l in (2, 3):
+            if step == PASS_STEP[l]:
+                for dy in range(1, 1 << (l - 1)):
+                    kv_along(l, dy).wait_recv()
+                    kv_pass(l, dy).start()
         if step in FIRST[1:]:
             l = FIRST.index(step)
-            for d in range(1, 1 << l):
-                kv_copy(l, d).wait_recv()
+            kv_sibling(l).wait_recv()
+            for dy in range(1, 1 << (l - 1)):
+                kv_pass(l, dy).wait_recv()
             transpose_kv(l)
         if step < BLOCKS:
             score_stage(step)
@@ -306,18 +391,20 @@
     dap[128:256, :] = mixed_b
     att[:, own_rows] = mixed_b.astype(F32).T.astype(BF16)
 
-    def a_copy(d):
-        return pltpu.make_async_remote_copy(
-            src_ref=att.at[:, own_rows],
-            dst_ref=att.at[:, own_rows],
-            send_sem=a_ss.at[d - 1],
-            recv_sem=a_rs.at[d - 1],
-            device_id=(seq, head_peer(d)),
-            device_id_type=MESH,
-        )
-
-    for d in range(1, nh):
-        a_copy(d).start()
+    a_sems = (a_ss, a_rs)
+
+    def a_own(i, half):
+        part = att.at[halves[half], own_rows]
+        return remote(part, part, a_sems, i + (0 if half == i else 2), (seq, sides[i]))
+
+    def a_pass(i):
+        part = att.at[halves[i], rows_of[1 - i]]
+        return remote(part, part, a_sems, 4 + i, (seq, sides[i]))
+
+    for i in range(2):
+        a_own(i, i).start()
+    for i in range(2):
+        a_own(i, 1 - i).start()
 
     rowt = iota((16, T), 0)
     hi, mid, lo = split3(joint)
@@ -325,11 +412,11 @@
         rowt, (hi[0:1], mid[0:1], lo[0:1], hi[1:2], mid[1:2], lo[1:2])
     ).astype(BF16)
 
-    for d in range(1, nh):
-        d_copy(d).wait_recv()
-    d_sum = dsend[own_rows, :].astype(F32)
-    for d in range(1, nh):
-        d_sum = d_sum + drecv[d - 1].astype(F32)
+    for i in range(2):
+        d_plain(i).wait_recv()
+    for i in range(2):
+        d_summed(i).wait_recv()
+    d_sum = dsend[own_rows, :].astype(F32) + drecv[0].astype(F32) + drecv[1].astype(F32)
     dap[0:128, :] = d_sum.astype(BF16)
 
     def prepare(b):
@@ -377,54 +464,87 @@
             dkv[:, 0:128] += d_k
             dkv[:, 128:256] += d_v
 
-    def g_copy(l, d):
+    g_sems = (gr_ss, gr_rs)
+    g_base = (0, 0, 1, 3)
+
+    def g_sibling(l):
+        to = gr1.at[0] if l == 1 else gother[l]
+        part = gsend[l].at[1 - core, 0] if l == 1 else gsend[l].at[1 - core]
+        return remote(part, to, g_sems, g_base[l], sibling)
+
+    def g_along(l, dy):
+        to = column(l, dy)
+        part = gtotal[l].at[lax.rem(to, 1 << (l - 1))]
+        return remote(part, grecv[l].at[dy - 1], g_sems, g_base[l] + dy, along(to))
+
+    def send_sibling(l):
         n = T >> l
-        i = slot(l, d)
-        part = lax.rem(rank[l] + d, 1 << l)
-        return pltpu.make_async_remote_copy(
-            src_ref=gsend[l].at[pl.ds(pl.multiple_of(part * n, n), n), :],
-            dst_ref=grecv[l].at[d - 1],
-            send_sem=gr_ss.at[i],
-            recv_sem=gr_rs.at[i],
-            device_id=(member(l, d), hx),
-            device_id_type=MESH,
-        )
-
-    groups = [[14], [12, 13], [8, 9, 10, 11], [0, 1, 2, 3], [4, 5, 6, 7]]
-    for b in groups[0]:
-        prepare(b)
-        grad_stage(b)
-    for i, group in enumerate(groups):
-        if i + 1 < len(groups):
-            for b in groups[i + 1]:
-                prepare(b)
-                grad_stage(b)
+        for i in range(1 << l):
+            gsend[l][i % 2, i // 2] = dkv[i * n : (i + 1) * n, :].astype(BF16)
+        g_sibling(l).start()
+        if l == 1:
+            own1[...] = dkv[block(rank[1], n), :]
+
+    def send_along(l):
+        g_sibling(l).wait_recv()
+        gtotal[l][...] = (gsend[l][core].astype(F32) + gother[l][...].astype(F32)).astype(BF16)
+        for dy in range(1, 1 << (l - 1)):
+            g_along(l, dy).start()
+
+    def stack_level(l):
+        for c in range(COUNT[l]):
+            rows = slice(c * C, (c + 1) * C)
+            if l == 1:
+                grad = own1[rows, :] + gr1[0, rows, :].astype(F32)
+            else:
+                grad = gtotal[l][lax.rem(y, 1 << (l - 1)), rows, :].astype(F32)
+                for dy in range(1, 1 << (l - 1)):
+                    grad = grad + grecv[l][dy - 1, rows, :].astype(F32)
+            stacks[l][c, 0:C, :] = jnp.where(kv_head1, 0.0, grad).astype(BF16)
+            stacks[l][c, C:256, :] = jnp.where(kv_head1, grad, 0.0).astype(BF16)
+
+    def finish_group(group):
         key_stage(group, group[0] != 4)
         for b in group:
             query_stage(b)
-        l = where[group[0]][0]
-        if l:
-            n = T >> l
-            gsend[l][...] = dkv[...].astype(BF16)
-            for d in range(1, 1 << l):
-                g_copy(l, d).start()
-            owns[l][...] = dkv[pl.ds(pl.multiple_of(rank[l] * n, n), n), :]
-
-    for d in range(1, nh):
-        a_copy(d).wait_recv()
+
+    def grad_group(group):
+        for b in group:
+            prepare(b)
+            grad_stage(b)
+
+    groups = [[14], [12, 13], [8, 9, 10, 11], [0, 1, 2, 3], [4, 5, 6, 7]]
+    grad_group(groups[0])
+    grad_group(groups[1])
+    finish_group(groups[0])
+    send_sibling(3)
+    grad_group(groups[2])
+    finish_group(groups[1])
+    send_sibling(2)
+    send_along(3)
+    grad_group(groups[3])
+    finish_group(groups[2])
+    send_sibling(1)
+    send_along(2)
+    for i in range(2):
+        a_own(i, i).wait_recv()
+        a_pass(i).start()
+    grad_group(groups[4])
+    finish_group(groups[3])
+    for i in range(2):
+        a_own(i, 1 - i).wait_recv()
+    for i in range(2):
+        a_pass(i).wait_recv()
+    for l in (3, 2):
+        for dy in range(1, 1 << (l - 1)):
+            g_along(l, dy).wait_recv()
+    g_sibling(1).wait_recv()
+    finish_group(groups[4])
+
     layer_ref[...] = nn(att[...], wfull[...]).astype(BF16)
 
     for l in (3, 2, 1):
-        for d in range(1, 1 << l):
-            g_copy(l, d).wait_recv()
-    for l in (3, 2, 1):
-        for c in range(COUNT[l]):
-            rows = slice(c * C, (c + 1) * C)
-            grad = owns[l][rows, :]
-            for d in range(1, 1 << l):
-                grad = grad + grecv[l][d - 1, rows, :].astype(F32)
-            stacks[l][c, 0:C, :] = jnp.where(kv_head1, 0.0, grad).astype(BF16)
-            stacks[l][c, C:256, :] = jnp.where(kv_head1, grad, 0.0).astype(BF16)
+        stack_level(l)
     for c in range(4):
         rows = slice(c * 256, (c + 1) * 256)
         place = side([sel1[...], sel2[c % 2 * 256 : c % 2 * 256 + 256, :], sel3[rows, :]])
@@ -441,12 +561,25 @@
 
     for d in range(1, nh):
         w_copy(d).wait_send()
-        d_copy(d).wait_send()
-        a_copy(d).wait_send()
+    for i in range(2):
+        for copy in (d_over(i), d_plain(i), d_summed(i), a_own(i, 0), a_own(i, 1), a_pass(i)):
+            copy.wait_send()
     for l in (1, 2, 3):
-        for d in range(1, 1 << l):
-            kv_copy(l, d).wait_send()
-            g_copy(l, d).wait_send()
+        kv_sibling(l).wait_send()
+        g_sibling(l).wait_send()
+        for dy in range(1, 1 << (l - 1)):
+            kv_along(l, dy).wait_send()
+            kv_pass(l, dy).wait_send()
+            g_along(l, dy).wait_send()
+
+
+def hand_out(*refs):
+    sems = refs[8]
+    copies = [pltpu.make_async_copy(refs[i], refs[4 + i], sems.at[i]) for i in range(4)]
+    for copy in copies:
+        copy.start()
+    for copy in copies:
+        copy.wait()
 
 
 def shards(nh, queries, key_rows, value_rows, offsets, w_out, d_out):
@@ -454,6 +587,9 @@
     dma = pltpu.SemaphoreType.DMA
     feat = 128 * nh
     scratch = [
+        *[pltpu.VMEM((T, 128), BF16)] * 3,
+        pltpu.VMEM((128, feat * 2), BF16),
+        pltpu.VMEM((T, 256), BF16),
         *[pltpu.VMEM((C << l, 256), BF16) for l in (1, 2, 3)],
         pltpu.VMEM((128, T), BF16),
         *[pltpu.VMEM((T, 256), BF16) for l in (1, 2, 3)],
@@ -466,39 +602,56 @@
         *[pltpu.VMEM((T >> l, 256), BF16) for l in (1, 2, 3)],
         pltpu.VMEM((feat, 256), BF16),
         pltpu.VMEM((feat, T), BF16),
-        pltpu.VMEM((max(nh - 1, 1), 128, T), BF16),
+        pltpu.VMEM((2, 128, 512), BF16),
+        pltpu.VMEM((2, 128, 512), BF16),
+        pltpu.VMEM((2, 128, T), BF16),
         pltpu.VMEM((272, T), BF16),
         pltpu.VMEM((LEVELS, 128, T), F32),
         pltpu.VMEM((LEVELS, 8, T), F32),
         pltpu.VMEM((T, feat), BF16),
         pltpu.VMEM((T, 256), F32),
         pltpu.VMEM((8, C, 128), F32),
-        *[pltpu.VMEM((T, 256), BF16) for l in (1, 2, 3)],
-        *[pltpu.VMEM(((1 << l) - 1, T >> l, 256), BF16) for l in (1, 2, 3)],
-        *[pltpu.VMEM((T >> l, 256), F32) for l in (1, 2, 3)],
+        *[pltpu.VMEM((2, (1 << l) // 2, T >> l, 256), BF16) for l in (1, 2, 3)],
+        *[pltpu.VMEM(((1 << l) // 2, T >> l, 256), BF16) for l in (2, 3)],
+        *[pltpu.VMEM(((1 << l) // 2, T >> l, 256), BF16) for l in (2, 3)],
+        *[pltpu.VMEM((max((1 << l) // 2 - 1, 1), T >> l, 256), BF16) for l in (1, 2, 3)],
+        pltpu.VMEM((T // 2, 256), F32),
         *[pltpu.VMEM((COUNT[l], 256, 256), BF16) for l in (1, 2, 3)],
         dma((11,)),
         dma((11,)),
-        dma((11,)),
-        dma((11,)),
-        *[dma((max(nh - 1, 1),))] * 6,
+        dma((7,)),
+        dma((7,)),
+        dma((nh - 1,)),
+        dma((nh - 1,)),
+        *[dma((6,))] * 4,
+        dma((5,)),
     ]
-    return pl.pallas_call(
+    outs = pl.pallas_call(
         functools.partial(kernel, nh),
         out_shape=(
-            jax.ShapeDtypeStruct((T, 256), BF16),
-            jax.ShapeDtypeStruct((T, 128), BF16),
-            jax.ShapeDtypeStruct((T, 128), BF16),
-            jax.ShapeDtypeStruct((T, 128), BF16),
+            pltpu.VMEM((T, 256), BF16),
+            pltpu.VMEM((T, 128), BF16),
+            pltpu.VMEM((T, 128), BF16),
+            pltpu.VMEM((T, 128), BF16),
         ),
-        in_specs=[pl.BlockSpec(memory_space=pltpu.SMEM)] + [vmem] * 5,
+        in_specs=[pl.BlockSpec(memory_space=pltpu.SMEM)] + [pl.BlockSpec(memory_space=pl.ANY)] * 5,
         out_specs=(vmem,) * 4,
         scratch_shapes=scratch,
         compiler_params=pltpu.CompilerParams(
             collective_id=0, has_side_effects=True, vmem_limit_bytes=56 * 1024 * 1024
         ),
         cost_estimate=pl.CostEstimate(flops=4_000_000_000, bytes_accessed=3_000_000, transcendentals=4_000_000),
-    )(offsets, queries, key_rows, value_rows, w_out, d_out)
+    )(offsets.T, queries, key_rows, value_rows, w_out, d_out)
+
+    anyspec = pl.BlockSpec(memory_space=pl.ANY)
+    outs = [pltpu.with_memory_space_constraint(x, pltpu.VMEM) for x in outs]
+    return pl.pallas_call(
+        hand_out,
+        out_shape=tuple(jax.ShapeDtypeStruct(x.shape, x.dtype) for x in outs),
+        in_specs=[vmem] * 4,
+        out_specs=(anyspec,) * 4,
+        scratch_shapes=[dma((4,))],
+    )(*outs)
 
 
 def solution(mesh):

time: 49.4 us -> 38.8 us (0.79)
  local copies, waits for them, and re-layouts: 6.04 us -> 0 us
  Pallas kernels: 42.5 us -> 37.6 us
    unnamed x11 -> x0, local copies, waits for them, and re-layouts: 6.04 us -> none
    pallas_call x1 -> x2, Pallas kernels: 42.5 us -> 37.6 us  [the longest x1 36.5 us: shards(): pl.pallas_call(functools.partial(kernel, nh), out_shape=(pltpu.VMEM((T, 2...]
where the time goes in v2:
time: 38.8 us; the launch traced here: 38.4 us
  Pallas kernels  37.6 us (97%)
  between operations  0.8 us (2%)
    pallas_call x1, Pallas kernels, shards(): pl.pallas_call(functools.partial(kernel, nh), out_shape=(pltpu.VMEM((T, 2...  36.5 us
    pallas_call x1, Pallas kernels, shards(): pl.pallas_call(hand_out, out_shape=tuple((jax.ShapeDtypeStruct(x.shape, x...  1.09 us

profile of v2, /device:TPU:1, one launch (start us, length us, event | category | flops | bytes accessed | tf_op | source)
XLA Modules:
  0.0 38.4 jit_solution(13872393663968715184)
XLA Ops:
  0.6 36.5 %shard_map.93 = (bf16[1024,256]{1,0:T(8,128)(2,1)S(1)}, bf16[1024,128]{1,0:T(8,128)(2,1)S(1)}, bf16[1024,128]{1,0:T(8,128)(2,1)S(1)}, bf16[1024,128]{1,0:T(8,128)(2,1)S(1)}) custom-call(s32[2,4]{1,0:T(2,128)} %bitcast.1, bf16[1024,128]{1,0:T(8,128)(2,1)} %q_hbm.1, bf16[1024,128]{1,0:T(8,128)(2,1)} %k_hbm.1, bf16[1024,128]{1,0:T(8,128)(2,1)} %v_hbm.1, ...), custom_call_target="tpu_custom_call" | custom-call | flops 4000000000 | bytes 3000000 | tf_op jit(solution)/shard_map/pallas_call | solution.py:629
  37.2 1.1 %shard_map.94 = (bf16[1024,256]{1,0:T(8,128)(2,1)}, bf16[1024,128]{1,0:T(8,128)(2,1)}, bf16[1024,128]{1,0:T(8,128)(2,1)}, bf16[1024,128]{1,0:T(8,128)(2,1)}) custom-call(bf16[1024,256]{1,0:T(8,128)(2,1)S(1)} %get-tuple-element.8.refs_0_, bf16[1024,128]{1,0:T(8,128)(2,1)S(1)} %get-tuple-element.9.refs_1_, bf16[1024,128]{1,0:T(8,128)(2,1)S(1)} %get-tuple-element.10.refs_2_, ...), custom_call_target="tpu_custom_call" | custom-call | tf_op jit(solution)/shard_map/pallas_call | solution.py:648

commit v3 on v2

--- a/solution.py
+++ b/solution.py
@@ -16,9 +16,9 @@
 COUNT = (8, 4, 2, 1)
 BLOCKS = 15
 F32, BF16 = jnp.float32, jnp.bfloat16
-W_STEP = 4
+W_STEP = 3
 D_STEP = 11
-PASS_STEP = (0, 0, 7, 9)
+PASS_STEP = (0, 0, 10, 12)
 
 
 def nn(a, b):

time: 38.8 us -> 37.9 us (0.977)
  Pallas kernels: 37.6 us -> 37 us
    pallas_call x1, Pallas kernels: 36.5 us -> 35.9 us  [shards(): pl.pallas_call(functools.partial(kernel, nh), out_shape=(pltpu.VMEM((T, 2...]
where the time goes in v3:
time: 37.9 us; the launch traced here: 37.8 us
  Pallas kernels  37 us (98%)
  between operations  0.8 us (2%)
    pallas_call x1, Pallas kernels, shards(): pl.pallas_call(functools.partial(kernel, nh), out_shape=(pltpu.VMEM((T, 2...  35.9 us
    pallas_call x1, Pallas kernels, shards(): pl.pallas_call(hand_out, out_shape=tuple((jax.ShapeDtypeStruct(x.shape, x...  1.09 us

profile of v3, /device:TPU:1, one launch (start us, length us, event | category | flops | bytes accessed | tf_op | source)
XLA Modules:
  0.0 37.8 jit_solution(7569684071726063454)
XLA Ops:
  0.6 35.9 %shard_map.93 = (bf16[1024,256]{1,0:T(8,128)(2,1)S(1)}, bf16[1024,128]{1,0:T(8,128)(2,1)S(1)}, bf16[1024,128]{1,0:T(8,128)(2,1)S(1)}, bf16[1024,128]{1,0:T(8,128)(2,1)S(1)}) custom-call(s32[2,4]{1,0:T(2,128)} %bitcast.1, bf16[1024,128]{1,0:T(8,128)(2,1)} %q_hbm.1, bf16[1024,128]{1,0:T(8,128)(2,1)} %k_hbm.1, bf16[1024,128]{1,0:T(8,128)(2,1)} %v_hbm.1, ...), custom_call_target="tpu_custom_call" | custom-call | flops 4000000000 | bytes 3000000 | tf_op jit(solution)/shard_map/pallas_call | solution.py:629
  36.6 1.1 %shard_map.94 = (bf16[1024,256]{1,0:T(8,128)(2,1)}, bf16[1024,128]{1,0:T(8,128)(2,1)}, bf16[1024,128]{1,0:T(8,128)(2,1)}, bf16[1024,128]{1,0:T(8,128)(2,1)}) custom-call(bf16[1024,256]{1,0:T(8,128)(2,1)S(1)} %get-tuple-element.8.refs_0_, bf16[1024,128]{1,0:T(8,128)(2,1)S(1)} %get-tuple-element.9.refs_1_, bf16[1024,128]{1,0:T(8,128)(2,1)S(1)} %get-tuple-element.10.refs_2_, ...), custom_call_target="tpu_custom_call" | custom-call | tf_op jit(solution)/shard_map/pallas_call | solution.py:648
